TPU v7x, 128 devices: a whole 4x4x4 slice. The times are simulated.
128 devices in a mesh: gz: 16 (over y, z), ta: 8 (over x, core).
Axes of the slice: x: 4, y: 4, z: 4, core: 2. Of those that a mesh axis runs over, the one named last changes fastest.
Arguments:
- potential: float32 [128, 128, 128, 128], P('ta', 'gz'), may hold values from -6 to 6
Outputs:
- propagator: float32 [128, 128, 128, 128], P('ta', 'gz')
All inputs are finite; a program needn't handle non-finite values.
Results may differ from a plain program's by a relative error of at most 0.000071.
Values sent between devices are 32-bit elements; how exact they have to be, the bound alone decides.
No kernel may reach another device: no remote copies, remote signals or barrier semaphores. Data moves between devices by JAX's collectives and lax.ppermute only.
A program may use at most 128 MiB of HBM per device.

v0:
```python
import math

import jax
import jax.numpy as jnp
from jax import lax
from jax.sharding import PartitionSpec as P


def tables(length):
    position = jnp.arange(length, dtype=jnp.int32)
    phase = position[:, None] * position[None, :] % length
    angle = phase.astype(jnp.float32) * (2.0 * math.pi / length)
    factor = 1.0 / math.sqrt(length)
    return (jnp.cos(angle) * factor, jnp.sin(angle) * factor)


def rotate(real_part, imag_part, form, length):
    cosine, sine = tables(length)
    highest = lax.Precision.HIGHEST
    real_cos = jnp.einsum(form, real_part, cosine, precision=highest)
    real_sin = jnp.einsum(form, real_part, sine, precision=highest)
    imag_cos = jnp.einsum(form, imag_part, cosine, precision=highest)
    imag_sin = jnp.einsum(form, imag_part, sine, precision=highest)
    return (real_cos + imag_sin, imag_cos - real_sin)


def spread_out(field, groups_z, groups_t):
    local_t, local_z, width_y, lanes = field.shape
    rows_y = width_y // (groups_z * groups_t)
    moved = jnp.transpose(field, (2, 0, 1, 3))
    moved = lax.all_to_all(moved, ("gz", "ta"), split_axis=0, concat_axis=0, tiled=True)
    moved = moved.reshape(groups_z, groups_t, rows_y, local_t, local_z, lanes)
    moved = jnp.transpose(moved, (1, 3, 0, 4, 2, 5))
    return moved.reshape(groups_t * local_t, groups_z * local_z, rows_y, lanes)


def bring_back(values, groups_z, groups_t):
    full_t, full_z, rows_y, lanes = values.shape
    local_t = full_t // groups_t
    local_z = full_z // groups_z
    blocks = values.reshape(groups_t, local_t, groups_z, local_z, rows_y, lanes)
    blocks = jnp.transpose(blocks, (2, 0, 1, 3, 4, 5))
    blocks = blocks.reshape(groups_z * groups_t * local_t, local_z, rows_y, lanes)
    return lax.all_to_all(blocks, ("gz", "ta"), split_axis=0, concat_axis=2, tiled=True)


def body(potential):
    local_t, local_z, width_y, width_x = potential.shape
    groups_z = lax.axis_size("gz")
    groups_t = lax.axis_size("ta")
    full_t = local_t * groups_t
    full_z = local_z * groups_z
    highest = lax.Precision.HIGHEST
    cosine, sine = tables(width_x)
    real_part = jnp.einsum("tzyx,xk->tzyk", potential, cosine, precision=highest)
    imag_part = -jnp.einsum("tzyx,xk->tzyk", potential, sine, precision=highest)
    real_part, imag_part = rotate(real_part, imag_part, "tzyx,yk->tzkx", width_y)
    joined = jnp.concatenate([real_part, imag_part], axis=-1)
    joined = spread_out(joined, groups_z, groups_t)
    real_part = joined[..., :width_x]
    imag_part = joined[..., width_x:]
    real_part, imag_part = rotate(real_part, imag_part, "tzyx,zk->tkyx", full_z)
    real_part, imag_part = rotate(real_part, imag_part, "tzyx,tk->kzyx", full_t)
    power = real_part * real_part + imag_part * imag_part
    return bring_back(power, groups_z, groups_t)


def solution(mesh):
    return jax.shard_map(
        body,
        mesh=mesh,
        in_specs=(P("ta", "gz", None, None),),
        out_specs=P("ta", "gz", None, None),
        check_vma=False,
    )
```

profile of v0, /device:TPU:1, one launch (start us, length us, event | category | flops | bytes accessed | tf_op | source)
XLA Modules:
  0.0 533.1 jit_solution(14759781932170274803)
XLA Ops:
  0.0 0.0 copy-start
  0.0 10.9 %fusion.35 = f32[128,16,8,128]{3,0,2,1:T(8,128)S(1)} fusion(f32[16,8,128,128]{3,2,1,0:T(8,128)} %param.1), kind=kOutput, calls=%fused_computation.40 | convolution fusion | flops 3221471232 | bytes 16777216 | tf_op jit(solution)/shard_map/tzyx,xk->tzyk/dot_general | solution.py:56
  10.9 0.0 copy-done
  10.9 7.6 %fusion.39 = f32[128,16,8,128]{3,0,2,1:T(8,128)S(1)} fusion(f32[16,8,128,128]{3,2,1,0:T(8,128)S(1)} %copy-done), kind=kOutput, calls=%fused_computation.44 | convolution fusion | flops 3221471232 | bytes 16777216 | tf_op jit(solution)/shard_map/tzyx,xk->tzyk/dot_general | solution.py:55
  18.6 8.4 %fusion = f32[128,16,8,128]{0,3,2,1:T(8,128)S(1)} fusion(f32[128,16,8,128]{3,0,2,1:T(8,128)S(1)} %fusion.35), kind=kOutput, calls=%fused_computation.3 | convolution fusion | flops 3223568384 | bytes 16777216 | tf_op jit(solution)/shard_map/tzyx,yk->tzkx/dot_general | solution.py:22
  27.0 9.4 %fusion.2 = f32[128,16,8,128]{0,3,2,1:T(8,128)} fusion(f32[128,16,8,128]{3,0,2,1:T(8,128)S(1)} %fusion.35), kind=kOutput, calls=%fused_computation.5 | convolution fusion | flops 3223568384 | bytes 16777216 | tf_op jit(solution)/shard_map/tzyx,yk->tzkx/dot_general | solution.py:23
  36.4 9.6 %add_bitcast_fusion.1 = f32[16,8,128,128]{2,3,1,0:T(8,128)S(1)} fusion(f32[128,16,8,128]{0,3,2,1:T(8,128)} %fusion.2, f32[128,16,8,128]{3,0,2,1:T(8,128)S(1)} %fusion.39), kind=kOutput, calls=%fused_computation.15 | convolution fusion | flops 3223568384 | bytes 25165824 | tf_op jit(solution)/shard_map/tzyx,yk->tzkx/dot_general | solution.py:20
  46.0 9.6 %subtract_bitcast_fusion.1 = f32[16,8,128,128]{2,3,1,0:T(8,128)} fusion(f32[128,16,8,128]{0,3,2,1:T(8,128)S(1)} %fusion, f32[128,16,8,128]{3,0,2,1:T(8,128)S(1)} %fusion.39), kind=kOutput, calls=%fused_computation.14 | convolution fusion | flops 3223568384 | bytes 25165824 | tf_op jit(solution)/shard_map/tzyx,yk->tzkx/dot_general | solution.py:21
  55.6 9.8 %maximum_bitcast_fusion = f32[128,16,8,256]{0,3,2,1:T(8,128)} fusion(f32[16,8,128,128]{2,3,1,0:T(8,128)} %subtract_bitcast_fusion.1, f32[16,8,128,128]{2,3,1,0:T(8,128)S(1)} %add_bitcast_fusion.1), kind=kLoop, calls=%fused_computation | loop fusion | flops 4194304 | bytes 33554432 | tf_op jit(solution)/shard_map/transpose | solution.py:30
  65.4 17.7 %copy.27 = f32[128,16,8,256]{3,2,1,0:T(8,128)} copy(f32[128,16,8,256]{0,3,2,1:T(8,128)} %maximum_bitcast_fusion) | data formatting | bytes 33554432 | tf_op jit(solution)/shard_map/transpose | solution.py:30
  83.1 199.4 %all_to_all.23 = f32[128,16,8,256]{3,2,1,0:T(8,128)} all-to-all(f32[128,16,8,256]{3,2,1,0:T(8,128)} %copy.27), channel_id=1, replica_groups=mesh['gz'=16,'ta'=8] {'gz','ta'}, dimensions={0} | all-to-all | bytes 33554432 | tf_op jit(solution)/shard_map/all_to_all | solution.py:31
  282.5 7.0 %copy.28 = f32[8,16,16,8,1,256]{5,3,2,1,0,4:T(8,128)S(1)} copy(f32[8,16,16,8,1,256]{5,3,1,0,2,4:T(8,128)} %bitcast.105) | data formatting | bytes 33554432 | tf_op jit(solution)/shard_map/transpose | solution.py:33
  289.6 10.0 %fusion.8 = f32[128,128,128]{2,0,1:T(8,128)} fusion(f32[128,128,1,256]{3,1,0,2:T(8,128)S(1)} %bitcast.101), kind=kOutput, calls=%fused_computation.16 | convolution fusion | flops 3221471232 | bytes 16777216 | tf_op jit(solution)/shard_map/tzyx,zk->tkyx/dot_general | solution.py:21
  299.6 10.3 %subtract_bitcast_fusion = f32[128,128,128]{2,1,0:T(8,128)S(1)} fusion(f32[128,128,128]{2,0,1:T(8,128)} %fusion.8, f32[128,128,1,256]{3,1,0,2:T(8,128)S(1)} %bitcast.102), kind=kOutput, calls=%fused_computation.12 | convolution fusion | flops 3223568384 | bytes 25165824 | tf_op jit(solution)/shard_map/tzyx,zk->tkyx/dot_general | solution.py:22
  309.9 17.4 %fusion.12 = f32[128,128,128]{2,0,1:T(8,128)} fusion(f32[128,128,128]{2,1,0:T(8,128)S(1)} %subtract_bitcast_fusion), kind=kOutput, calls=%fused_computation.20 | convolution fusion | flops 3221471232 | bytes 16777216 | tf_op jit(solution)/shard_map/tzyx,tk->kzyx/dot_general | solution.py:22
  327.3 17.1 %fusion.14 = f32[128,128,128]{2,0,1:T(8,128)} fusion(f32[128,128,128]{2,1,0:T(8,128)S(1)} %subtract_bitcast_fusion), kind=kOutput, calls=%fused_computation.22 | convolution fusion | flops 3221471232 | bytes 16777216 | tf_op jit(solution)/shard_map/tzyx,tk->kzyx/dot_general | solution.py:23
  344.4 9.9 %fusion.9 = f32[128,128,128]{2,0,1:T(8,128)} fusion(f32[128,128,1,256]{3,1,0,2:T(8,128)S(1)} %bitcast.103), kind=kOutput, calls=%fused_computation.17 | convolution fusion | flops 3221471232 | bytes 16777216 | tf_op jit(solution)/shard_map/tzyx,zk->tkyx/dot_general | solution.py:20
  354.3 11.4 %add_bitcast_fusion = f32[128,128,128]{2,1,0:T(8,128)S(1)} fusion(f32[128,128,128]{2,0,1:T(8,128)} %fusion.9, f32[128,128,1,256]{3,1,0,2:T(8,128)S(1)} %bitcast.104), kind=kOutput, calls=%fused_computation.13 | convolution fusion | flops 3223568384 | bytes 25165824 | tf_op jit(solution)/shard_map/tzyx,zk->tkyx/dot_general | solution.py:23
  365.7 16.9 %fusion.16 = f32[128,128,128]{2,0,1:T(8,128)} fusion(f32[128,128,128]{2,1,0:T(8,128)S(1)} %add_bitcast_fusion), kind=kOutput, calls=%fused_computation.24 | convolution fusion | flops 3221471232 | bytes 16777216 | tf_op jit(solution)/shard_map/tzyx,tk->kzyx/dot_general | solution.py:21
  382.6 23.9 %multiply_add_fusion = f32[128,128,128]{2,0,1:T(8,128)} fusion(f32[128,128,128]{2,0,1:T(8,128)} %fusion.12, f32[128,128,128]{2,0,1:T(8,128)} %fusion.16, f32[128,128,128]{2,0,1:T(8,128)} %fusion.14, f32[128,128,128]{2,1,0:T(8,128)S(1)} %add_bitcast_fusion), kind=kOutput, calls=%fused_computation.11 | convolution fusion | flops 3231956992 | bytes 41943040 | tf_op jit(solution)/shard_map/tzyx,tk->kzyx/dot_general | solution.py:20
  406.5 10.0 %copy.33 = f32[8,16,16,8,1,128]{5,3,1,0,2,4:T(8,128)S(1)} copy(f32[8,16,16,8,1,128]{5,1,0,3,2,4:T(8,128)} %bitcast.106) | data formatting | bytes 16777216 | tf_op jit(solution)/shard_map/reshape | solution.py:41
  416.4 108.1 %all_to_all.24 = f32[2048,8,1,128]{3,1,2,0:T(8,128)S(1)} all-to-all(f32[2048,8,1,128]{3,1,2,0:T(8,128)S(1)} %bitcast.107), channel_id=1, replica_groups=mesh['gz'=16,'ta'=8] {'gz','ta'}, dimensions={0} | all-to-all | bytes 16777216 | tf_op jit(solution)/shard_map/all_to_all | solution.py:44
  524.6 8.3 %copy.35 = f32[16,8,128,128]{3,2,1,0:T(8,128)} copy(f32[16,8,128,128]{3,1,0,2:T(8,128)S(1)} %bitcast.108) | data formatting | bytes 16777216 | tf_op jit(solution)/shard_map/all_to_all | solution.py:44
Async XLA Ops:
  0.0 10.9 %copy-start = (f32[16,8,128,128]{3,2,1,0:T(8,128)S(1)}, f32[16,8,128,128]{3,2,1,0:T(8,128)}, u32[]{:S(2)}) copy-start(f32[16,8,128,128]{3,2,1,0:T(8,128)} %param.1) | copy-start | bytes 25165828
where the time goes:
time: 542 us; the launch traced here: 533 us
  blocking collectives  308 us (57%)
  matrix products  172 us (32%)
  local copies, waits for them, and re-layouts  42.9 us (8%)
  other arithmetic  9.83 us (2%)
    all_to_all x1, blocking collectives, spread_out(): lax.all_to_all(moved, ('gz', 'ta'), split_axis=0, concat_axis=0, tiled=True)  199 us
    all_to_all x1, blocking collectives, bring_back(): lax.all_to_all(blocks, ('gz', 'ta'), split_axis=0, concat_axis=2, tiled=T...  108 us
    dot_general x3, matrix products, rotate(): real_cos = jnp.einsum(form, real_part, cosine, precision=highest)  43.3 us
    dot_general x3, matrix products, rotate(): imag_sin = jnp.einsum(form, imag_part, sine, precision=highest)  37.8 us
    dot_general x3, matrix products, rotate(): real_sin = jnp.einsum(form, real_part, sine, precision=highest)  36.6 us
    dot_general x3, matrix products, rotate(): imag_cos = jnp.einsum(form, imag_part, cosine, precision=highest)  36.1 us
    transpose x1, local copies, waits for them, and re-layouts, spread_out(): moved = jnp.transpose(field, (2, 0, 1, 3))  17.7 us
    dot_general x1, matrix products, body(): imag_part = -jnp.einsum('tzyx,xk->tzyk', potential, sine, precision=highest)  10.9 us

commit v1 on v0

v1 whole, which is shorter than its diff:
```python
import math

import ml_dtypes
import numpy as np

import jax
import jax.numpy as jnp
from jax import lax
from jax.experimental import pallas as pl
from jax.experimental.pallas import tpu as pltpu
from jax.sharding import PartitionSpec as P

N = 128
H = 64
AXES = ("gz", "ta")
BF = jnp.bfloat16
F32 = jnp.float32


def split_np(w):
    hi = w.astype(ml_dtypes.bfloat16)
    lo = (w - hi.astype(np.float64)).astype(ml_dtypes.bfloat16)
    return hi, lo


def angles():
    k = np.arange(N)
    phase = np.outer(k, k) % N
    c = np.cos(2 * np.pi * phase / N)
    s = np.sin(2 * np.pi * phase / N)
    quarter = phase % (N // 4) == 0
    c[quarter] = np.round(c[quarter])
    s[quarter] = np.round(s[quarter])
    return c, s


def table_x():
    c, s = angles()
    w = np.concatenate([c[:, :H], -s[:, :H]], axis=1)
    w[:, H] = c[:, H]
    hi, lo = split_np(w / N)
    row = np.concatenate([hi, lo], axis=1)
    return np.concatenate([row, row], axis=0)


def table_full(scale):
    c, s = angles()
    hi, lo = split_np(np.concatenate([c, s], axis=0) * scale)
    hi = np.concatenate([hi, hi], axis=1)
    lo = np.concatenate([lo, lo], axis=1)
    return np.concatenate([hi, lo], axis=0)


def split(x):
    hi = x.astype(BF)
    lo = (x - hi.astype(F32)).astype(BF)
    return hi, lo


def stacked(parts):
    his, los = zip(*[split(p) for p in parts])
    return jnp.concatenate([jnp.concatenate(his, axis=1), jnp.concatenate(los, axis=1)], axis=0)


def cos_sin(table, parts):
    out = jnp.dot(table, stacked(parts), preferred_element_type=F32)
    rows = table.shape[0] // 2
    out = out[:rows] + out[rows:]
    half = rows // 2
    return [(out[:half, N * i : N * i + N], out[half:, N * i : N * i + N]) for i in range(2)]


def lane_of(shape):
    return lax.broadcasted_iota(jnp.int32, shape, 1)


def xy_kernel(x_ref, wx_ref, wy_ref, o_ref):
    planes = x_ref.shape[1]
    x = x_ref[0].reshape(planes * N, N)
    hi, lo = split(x)
    r = jnp.dot(jnp.concatenate([hi, lo], axis=1), wx_ref[...], preferred_element_type=F32)
    r = r[:, :N] + r[:, N:]
    lane = lane_of((N, N))
    row = lax.broadcasted_iota(jnp.int32, (N, N), 0)
    late = row > H
    sign = jnp.where(lane < H, 1.0, -1.0).astype(F32)
    swap = (lane == H) & late
    keep = jnp.where((lane == 0) & late, 0.0, jnp.where((lane == H) & (row % H != 0), 0.0, 1.0)).astype(F32)
    roll = jnp.where((lane == 0) & ~late, 0.0, sign).astype(F32)
    for z in range(0, planes, 2):
        for i, (p, q) in enumerate(cos_sin(wy_ref[...], [r[N * z : N * z + N], r[N * z + N : N * z + 2 * N]])):
            turned = pltpu.roll(jnp.where(swap, p, q), H, 1)
            a = jnp.where(swap, -q, p * keep + turned * roll)
            o_ref[:, 0, z + i, :] = a


def xy_transform(potential):
    t, z, _, _ = potential.shape
    return pl.pallas_call(
        xy_kernel,
        grid=(t,),
        in_specs=[
            pl.BlockSpec((1, z, N, N), lambda i: (i, 0, 0, 0)),
            pl.BlockSpec((2 * N, 2 * N), lambda i: (0, 0)),
            pl.BlockSpec((4 * N, 2 * N), lambda i: (0, 0)),
        ],
        out_specs=pl.BlockSpec((N, 1, z, N), lambda i: (0, i, 0, 0)),
        out_shape=jax.ShapeDtypeStruct((N, t, z, N), F32),
        compiler_params=pltpu.CompilerParams(vmem_limit_bytes=40 * 2**20),
    )(potential, jnp.asarray(table_x()), jnp.asarray(table_full(1.0)))


def z_kernel(x_ref, w_ref, o_ref):
    g, _, rows, z, _ = x_ref.shape
    sign = jnp.where(lane_of((N, N)) < H, 1.0, -1.0).astype(F32)
    for t in range(0, rows, 2):
        parts = [x_ref[:, 0, t + i].reshape(g * z, N) for i in range(2)]
        for i, (p, q) in enumerate(cos_sin(w_ref[...], parts)):
            o_ref[:, 0, t + i, :] = p + pltpu.roll(q, H, 1) * sign


def z_transform(field, gz, ta):
    _, t, z, _ = field.shape
    field = field.reshape(gz, ta, t, z, N)
    return pl.pallas_call(
        z_kernel,
        grid=(ta,),
        in_specs=[
            pl.BlockSpec((gz, 1, t, z, N), lambda i: (0, i, 0, 0, 0)),
            pl.BlockSpec((4 * N, 2 * N), lambda i: (0, 0)),
        ],
        out_specs=pl.BlockSpec((N, 1, t, N), lambda i: (0, i, 0, 0)),
        out_shape=jax.ShapeDtypeStruct((N, ta, t, N), F32),
        compiler_params=pltpu.CompilerParams(vmem_limit_bytes=40 * 2**20),
    )(field, jnp.asarray(table_full(1.0 / N)))


def t_kernel(y_ref, w_ref, o_ref):
    gz, _, planes, _ = o_ref.shape
    me = lax.axis_index("gz") * lax.axis_size("ta") + lax.axis_index("ta")
    lane = lane_of((N, N))
    sign = jnp.where(lane < H, 1.0, -1.0).astype(F32)
    edge = (lane == 0) | (lane == H)
    own = edge & ((me == 0) | (me == H))
    late = edge & (me > H)
    first = (lane < H) ^ late
    same = jnp.where(own, 0.5, 1.0).astype(F32)
    mixed = jnp.where(own, 0.5 * sign, 0.0).astype(F32)
    same_b = jnp.where(own, -0.5 * sign, 1.0).astype(F32)
    mixed_b = jnp.where(own, 0.5, 0.0).astype(F32)

    def power(plus, minus):
        a = plus * same + minus * mixed
        b = plus * mixed_b + minus * same_b
        a = a * a
        b = b * b
        return jnp.where(first, a, b) + pltpu.roll(jnp.where(first, b, a), H, 1)

    def step(g, carry):
        for j in range(planes):
            kz = g * planes + j
            other = jnp.where(kz == 0, N // 2, N - kz)
            parts = [y_ref[kz], y_ref[other]]
            (pa, qa), (pb, qb) = cos_sin(w_ref[...], parts)
            qa = pltpu.roll(qa, H, 1) * sign
            qb = pltpu.roll(qb, H, 1) * sign
            minus_a, minus_b = pa - qa, pb - qb
            if j == 0:
                alone = g == 0
                minus_a, minus_b = jnp.where(alone, minus_b, minus_a), jnp.where(alone, minus_a, minus_b)
                there = jnp.where(alone, gz // 2, gz - g)
                slot = 0
            else:
                there = gz - 1 - g
                slot = planes - j
            o_ref[g, :, j, :] = power(pa + qa, minus_b)
            o_ref[there, :, slot, :] = power(pb + qb, minus_a)
        return carry

    lax.fori_loop(0, gz // 2, step, 0)


def t_transform(y, gz, planes):
    return pl.pallas_call(
        t_kernel,
        in_specs=[pl.BlockSpec(memory_space=pltpu.VMEM)] * 2,
        out_specs=pl.BlockSpec(memory_space=pltpu.VMEM),
        out_shape=jax.ShapeDtypeStruct((gz, N, planes, N), F32),
        compiler_params=pltpu.CompilerParams(vmem_limit_bytes=40 * 2**20),
    )(y.reshape(N, N, N), jnp.asarray(table_full(1.0)))


def join_kernel(x_ref, o_ref):
    z = x_ref.shape[2]
    lane = lane_of((z, N))
    back = (N + H - lane) % N
    for s in range(N):
        here = x_ref[s, 0]
        there = jnp.take_along_axis(x_ref[(N - s) % N, 0], back, axis=1)
        if s == 0 or s == H:
            mine = lane <= H
        elif s < H:
            mine = lane < H
        else:
            mine = (lane <= H) & (lane > 0)
        o_ref[0, :, s, :] = jnp.where(mine, here, there)


def join(received):
    _, t, z, _ = received.shape
    return pl.pallas_call(
        join_kernel,
        grid=(t,),
        in_specs=[pl.BlockSpec((N, 1, z, N), lambda i: (0, i, 0, 0))],
        out_specs=pl.BlockSpec((1, z, N, N), lambda i: (i, 0, 0, 0)),
        out_shape=jax.ShapeDtypeStruct((t, z, N, N), F32),
        compiler_params=pltpu.CompilerParams(vmem_limit_bytes=40 * 2**20),
    )(received)


def body(potential):
    t, z, _, _ = potential.shape
    gz = lax.axis_size("gz")
    ta = lax.axis_size("ta")
    sent = xy_transform(potential)
    field = lax.all_to_all(sent, AXES, split_axis=0, concat_axis=0, tiled=True)
    y = z_transform(field, gz, ta)
    power = t_transform(y, gz, z)
    power = power.reshape(gz * ta, t, z, N)
    received = lax.all_to_all(power, AXES, split_axis=0, concat_axis=0, tiled=True)
    return join(received)


def solution(mesh):
    return jax.shard_map(
        body,
        mesh=mesh,
        in_specs=(P("ta", "gz", None, None),),
        out_specs=P("ta", "gz", None, None),
        check_vma=False,
    )
```

time: 542 us -> 278 us (0.51); the launches traced: 533 us -> 277 us
  matrix products: 172 us -> 0 us
  blocking collectives: 308 us -> 214 us
  Pallas kernels: 0 us -> 58.1 us
  local copies, waits for them, and re-layouts: 42.9 us -> 5.26 us
  other arithmetic: 9.83 us -> 0 us
    dot_general x14 -> x0, matrix products: 172 us -> none  [the longest x3 43.3 us: rotate(): real_cos = jnp.einsum(form, real_part, cosine, precision=highest)]
    all_to_all x2, blocking collectives: 308 us -> 214 us  [the longest x1 109 us: body(): field = lax.all_to_all(sent, AXES, split_axis=0, concat_axis=0, tiled=True)]
    pallas_call x0 -> x4, Pallas kernels: none -> 58.1 us  [the longest x1 18.7 us: t_transform(): pl.pallas_call(t_kernel, in_specs=[pl.BlockSpec(memory_space=pltpu.VMEM)]...]
    transpose x2 -> x0, local copies, waits for them, and re-layouts: 24.7 us -> none  [the longest x1 17.7 us: spread_out(): moved = jnp.transpose(field, (2, 0, 1, 3))]
    reshape x1 -> x0, local copies, waits for them, and re-layouts: 9.95 us -> none  [bring_back(): blocks = values.reshape(groups_t, local_t, groups_z, local_z, rows_y, lanes)]
    transpose x1 -> x0, other arithmetic: 9.83 us -> none  [spread_out(): moved = jnp.transpose(field, (2, 0, 1, 3))]
    all_to_all x1 -> x0, local copies, waits for them, and re-layouts: 8.25 us -> none  [bring_back(): lax.all_to_all(blocks, ('gz', 'ta'), split_axis=0, concat_axis=2, tiled=T...]
where the time goes in v1:
time: 278 us; the launch traced here: 277 us
  blocking collectives  214 us (77%)
  Pallas kernels  58.1 us (21%)
  local copies, waits for them, and re-layouts  5.26 us (2%)
    all_to_all x1, blocking collectives, body(): field = lax.all_to_all(sent, AXES, split_axis=0, concat_axis=0, tiled=True)  109 us
    all_to_all x1, blocking collectives, body(): lax.all_to_all(power, AXES, split_axis=0, concat_axis=0, tiled=True)  105 us
    pallas_call x1, Pallas kernels, t_transform(): pl.pallas_call(t_kernel, in_specs=[pl.BlockSpec(memory_space=pltpu.VMEM)]...  18.7 us
    pallas_call x1, Pallas kernels, xy_transform(): pl.pallas_call(xy_kernel, grid=(t,), in_specs=[pl.BlockSpec((1, z, N, N),...  17.8 us
    pallas_call x1, Pallas kernels, z_transform(): pl.pallas_call(z_kernel, grid=(ta,), in_specs=[pl.BlockSpec((gz, 1, t, z,...  11.2 us
    pallas_call x1, Pallas kernels, join(): pl.pallas_call(join_kernel, grid=(t,), in_specs=[pl.BlockSpec((N, 1, z, N...  10.4 us

profile of v1, /device:TPU:1, one launch (start us, length us, event | category | flops | bytes accessed | tf_op | source)
XLA Modules:
  0.0 277.2 jit_solution(15945725410703329046)
XLA Ops:
  0.0 0.0 copy-start.1
  0.0 0.9 copy-done.1
  1.0 0.0 copy-start.4
  1.0 0.9 copy-done.4
  1.9 17.8 %shard_map.55 = f32[128,16,8,128]{3,2,1,0:T(8,128)S(1)} custom-call(f32[16,8,128,128]{3,2,1,0:T(8,128)} %x_ref.1, bf16[256,256]{1,0:T(8,128)(2,1)S(1)} %copy-done.4, bf16[512,256]{1,0:T(8,128)(2,1)S(1)} %copy-done.1), custom_call_target="tpu_custom_call" | custom-call | tf_op jit(solution)/shard_map/pallas_call | solution.py:99
  19.6 0.0 copy-start.3
  19.6 109.3 %all_to_all.10 = f32[128,16,8,128]{3,2,1,0:T(8,128)} all-to-all(f32[128,16,8,128]{3,2,1,0:T(8,128)S(1)} %shard_map.55), channel_id=1, replica_groups=mesh['gz'=16,'ta'=8] {'gz','ta'}, dimensions={0} | all-to-all | bytes 16777216 | tf_op jit(solution)/shard_map/all_to_all | solution.py:226
  129.0 0.0 copy-done.3
  129.0 0.0 copy-start.2
  129.0 11.2 %shard_map.56 = f32[128,8,16,128]{3,2,1,0:T(8,128)S(1)} custom-call(f32[16,8,16,8,128]{4,3,2,1,0:T(8,128)} %bitcast.5, bf16[512,256]{1,0:T(8,128)(2,1)S(1)} %copy-done.3), custom_call_target="tpu_custom_call" | custom-call | tf_op jit(solution)/shard_map/pallas_call | solution.py:125
  140.2 0.0 copy-start
  140.2 3.4 %copy-done = f32[128,8,16,128]{3,2,1,0:T(8,128)} copy-done((f32[128,8,16,128]{3,2,1,0:T(8,128)}, f32[128,8,16,128]{3,2,1,0:T(8,128)S(1)}, u32[]{:S(2)}) %copy-start) | copy-done | bytes 8388632
  143.6 0.0 copy-done.2
  143.6 18.7 %shard_map.57 = f32[16,128,8,128]{3,2,1,0:T(8,128)S(1)} custom-call(f32[128,128,128]{2,1,0:T(8,128)} %bitcast.3, bf16[512,256]{1,0:T(8,128)(2,1)S(1)} %copy-done.2), custom_call_target="tpu_custom_call" | custom-call | tf_op jit(solution)/shard_map/pallas_call | solution.py:184
  162.2 104.5 %all_to_all.11.x_ref = f32[128,16,8,128]{3,2,1,0:T(8,128)S(1)} all-to-all(f32[128,16,8,128]{3,2,1,0:T(8,128)S(1)} %bitcast.4), channel_id=1, replica_groups=mesh['gz'=16,'ta'=8] {'gz','ta'}, dimensions={0} | all-to-all | bytes 16777216 | tf_op jit(solution)/shard_map/all_to_all | solution.py:230
  266.8 10.4 %shard_map.58 = f32[16,8,128,128]{3,2,1,0:T(8,128)} custom-call(f32[128,16,8,128]{3,2,1,0:T(8,128)S(1)} %all_to_all.11.x_ref), custom_call_target="tpu_custom_call" | custom-call | tf_op jit(solution)/shard_map/pallas_call | solution.py:211
Async XLA Ops:
  0.0 0.9 copy-start.1
  1.0 0.9 copy-start.4
  19.6 109.4 %copy-start.3 = (bf16[512,256]{1,0:T(8,128)(2,1)S(1)}, bf16[512,256]{1,0:T(8,128)(2,1)}, u32[]{:S(2)}) copy-start(bf16[512,256]{1,0:T(8,128)(2,1)} %constant.8.clone.w_ref) | copy-start | bytes 786436
  129.0 14.6 %copy-start.2 = (bf16[512,256]{1,0:T(8,128)(2,1)S(1)}, bf16[512,256]{1,0:T(8,128)(2,1)}, u32[]{:S(2)}) copy-start(bf16[512,256]{1,0:T(8,128)(2,1)} %constant.7.clone.wy_ref.w_ref) | copy-start | bytes 786436
  140.2 3.4 %copy-start = (f32[128,8,16,128]{3,2,1,0:T(8,128)}, f32[128,8,16,128]{3,2,1,0:T(8,128)S(1)}, u32[]{:S(2)}) copy-start(f32[128,8,16,128]{3,2,1,0:T(8,128)S(1)} %shard_map.56) | copy-start | bytes 25165828

commit v2 on v0

v2 whole, which is shorter than its diff:
```python
import ml_dtypes
import numpy as np

import jax
import jax.numpy as jnp
from jax import lax
from jax.experimental import pallas as pl
from jax.experimental.pallas import tpu as pltpu
from jax.sharding import PartitionSpec as P

N = 128
H = 64
AXES = ("gz", "ta")
BF = jnp.bfloat16
F32 = jnp.float32
MIB = 2**20
ROOT = float(np.sqrt(0.5))


def split_np(w):
    hi = w.astype(ml_dtypes.bfloat16)
    lo = (w - hi.astype(np.float64)).astype(ml_dtypes.bfloat16)
    return hi, lo


def angles():
    k = np.arange(N)
    phase = np.outer(k, k) % N
    c = np.cos(2 * np.pi * phase / N)
    s = np.sin(2 * np.pi * phase / N)
    quarter = phase % (N // 4) == 0
    c[quarter] = np.round(c[quarter])
    s[quarter] = np.round(s[quarter])
    return c, s


def table_x():
    c, s = angles()
    w = np.concatenate([c[:, :H], -s[:, :H]], axis=1)
    w[:, H] = c[:, H]
    hi, lo = split_np(w / N)
    row = np.concatenate([hi, lo], axis=1)
    return np.concatenate([row, row], axis=0)


def table_z():
    c, s = angles()
    hi, lo = split_np(np.concatenate([c[: H + 1], s[1:H]], axis=0) / N)
    return np.concatenate([hi, hi, lo, lo], axis=1)


def split(x):
    hi = x.astype(BF)
    lo = (x - hi.astype(F32)).astype(BF)
    return hi, lo


def add(a, b):
    im = b[1] if a[1] is None else a[1] if b[1] is None else a[1] + b[1]
    return a[0] + b[0], im


def sub(a, b):
    im = a[1] if b[1] is None else -b[1] if a[1] is None else a[1] - b[1]
    return a[0] - b[0], im


def conj(a):
    return a[0], None if a[1] is None else -a[1]


def turn_by(a, k, n):
    k = k % n
    re, im = a
    if k == 0:
        return a
    if 4 * k == n:
        return jnp.zeros_like(re) if im is None else im, -re
    if im is None:
        angle = 2 * np.pi * k / n
        return re * float(np.cos(angle)), re * float(-np.sin(angle))
    if 8 * k == n:
        return (re + im) * ROOT, (im - re) * ROOT
    if 8 * k == 3 * n:
        return (im - re) * ROOT, (re + im) * -ROOT
    c, s = float(np.cos(2 * np.pi * k / n)), float(np.sin(2 * np.pi * k / n))
    return re * c + im * s, im * c - re * s


def transform(x):
    n = len(x)
    if n == 1:
        return x
    even, odd = transform(x[0::2]), transform(x[1::2])
    out = [None] * n
    for k in range(n // 2):
        t = turn_by(odd[k], k, n)
        out[k], out[k + n // 2] = add(even[k], t), sub(even[k], t)
    return out


def transform_real(x):
    n = len(x)
    if n == 1:
        return [(x[0], None)]
    if n == 2:
        return [(x[0] + x[1], None), (x[0] - x[1], None)]
    even, odd = transform_real(x[0::2]), transform_real(x[1::2])
    out = [None] * (n // 2 + 1)
    out[0], out[n // 2] = add(even[0], odd[0]), sub(even[0], odd[0])
    for k in range(1, n // 4):
        t = turn_by(odd[k], k, n)
        out[k], out[n // 2 - k] = add(even[k], t), conj(sub(even[k], t))
    out[n // 4] = (even[n // 4][0], -odd[n // 4][0])
    return out


def lane_of(shape):
    return lax.broadcasted_iota(jnp.int32, shape, 1)


def xy_kernel(x_ref, w_ref, o_ref, x_buf, f_buf, h_buf, x_sem):
    steps, planes = x_ref.shape[:2]
    slots = x_buf.shape[0]
    lane = lane_of((planes, N))
    keep = jnp.where(lane == H, 0.0, 1.0).astype(F32)
    turn = jnp.where(lane == 0, 0.0, jnp.where(lane < H, -1.0, 1.0)).astype(F32)
    keep_back = jnp.where(lane == 0, 0.0, 1.0).astype(F32)
    turn_back = jnp.where(lane < H, 1.0, -1.0).astype(F32)
    edge = lane == H

    def fetch(t, slot):
        return [
            pltpu.make_async_copy(x_ref.at[t, z], x_buf.at[slot, :, z, :], x_sem.at[slot, z])
            for z in range(planes)
        ]

    for t in range(slots):
        for copy in fetch(t, t):
            copy.start()

    def step(t, carry):
        slot = lax.rem(t, slots)
        for copy in fetch(t, slot):
            copy.wait()
        for b in range(8):
            for c, v in enumerate(transform_real([x_buf[slot, 8 * a + b] for a in range(16)])):
                re, im = turn_by(v, b * c, N)
                h_buf[0, c, b] = re
                if im is not None:
                    h_buf[1, c, b] = im
        for c in range(9):
            real = c == 0
            parts = []
            for b in range(8):
                flat = real or (c == 8 and b == 0)
                parts.append((h_buf[0, c, b], None if flat else h_buf[1, c, b]))
            if real:
                parts = transform_real([v[0] for v in parts])
            else:
                parts = transform(parts)
            for d, v in enumerate(parts):
                ky = c + 16 * d
                if c == 8 and d >= 4:
                    continue
                re, im = v
                if ky > H:
                    ky, im = N - ky, -im
                f_buf[ky] = re
                if ky % H:
                    f_buf[H + ky] = im

        @pl.when(t + slots < steps)
        def _():
            for copy in fetch(t + slots, slot):
                copy.start()

        hi, lo = split(f_buf[...].reshape(N * planes, N))
        r = jnp.dot(jnp.concatenate([hi, lo], axis=1), w_ref[...], preferred_element_type=F32)
        r = (r[:, :N] + r[:, N:]).reshape(N, planes, N)
        o_ref[0, t] = r[0]
        o_ref[H, t] = r[H]
        for i in range(1, H):
            p, q = r[i], r[H + i]
            turned = pltpu.roll(jnp.where(edge, p, q), H, 1)
            o_ref[i, t] = p * keep + turned * turn
            o_ref[H + i, t] = jnp.where(edge, -q, p * keep_back + turned * turn_back)
        return carry

    lax.fori_loop(0, steps, step, 0)


def xy_transform(potential):
    t, z, _, _ = potential.shape
    slots = 6
    return pl.pallas_call(
        xy_kernel,
        in_specs=[pl.BlockSpec(memory_space=pltpu.HBM), pl.BlockSpec(memory_space=pltpu.VMEM)],
        out_specs=pl.BlockSpec(memory_space=pltpu.VMEM),
        out_shape=jax.ShapeDtypeStruct((N, t, z, N), F32),
        scratch_shapes=[
            pltpu.VMEM((slots, N, z, N), F32),
            pltpu.VMEM((N, z, N), F32),
            pltpu.VMEM((2, 9, 8, z, N), F32),
            pltpu.SemaphoreType.DMA((slots, z)),
        ],
        compiler_params=pltpu.CompilerParams(vmem_limit_bytes=48 * MIB),
    )(potential, jnp.asarray(table_x()))


def zt_kernel(x_ref, w_ref, o_ref, y_ref):
    gz, times, planes, _ = x_ref.shape
    groups = gz // 2
    me = lax.axis_index("gz") * lax.axis_size("ta") + lax.axis_index("ta")
    lane = lane_of((1, N))
    first = lane < H
    paired = (me == 0) | (me == H)
    late = me > H
    low, high = lane == 0, lane == H
    u_p = jnp.where(high & late, -1.0, 1.0).astype(F32)
    u_q = jnp.where((low | high) & paired, 0.0, jnp.where(low & late, -1.0, 1.0)).astype(F32)
    v_p = jnp.where((low | high) & paired, 0.0, jnp.where(low & late, -1.0, 1.0)).astype(F32)
    v_q = jnp.where(high & (paired | late), -1.0, 1.0).astype(F32)
    flip = jnp.where((low | high) & late, -1.0, 1.0).astype(F32)
    top = lax.broadcasted_iota(jnp.int32, (planes, N), 0) == 0
    first_8 = lane_of((planes, N)) < H
    edge_8 = (lane_of((planes, N)) == 0) | (lane_of((planes, N)) == H)
    own_8 = edge_8 & paired
    own_top = own_8 & top
    straight = first_8 | own_8

    def z_step(n, carry):
        for m in range(0, 8, 2):
            his, los = zip(*[split(x_ref[:, 8 * n + m + i].reshape(gz * planes, N)) for i in range(2)])
            hi, lo = jnp.concatenate(his, axis=1), jnp.concatenate(los, axis=1)
            out = jnp.dot(w_ref[...], jnp.concatenate([hi, lo, hi, lo], axis=0), preferred_element_type=F32)
            for i in range(2):
                t = 8 * n + m + i
                p, q = out[:H, N * i : N * i + N], out[H:, N * i : N * i + N]
                rp, rq = pltpu.roll(p, H, 1), pltpu.roll(q, H, 1)
                u, v = p * u_p + rq * u_q, rp * v_p - q * v_q
                re, im = jnp.where(first, u, v), jnp.where(first, v, u)
                y_ref[0, :, t] = re.reshape(groups, planes, N)
                y_ref[1, :, t] = im.reshape(groups, planes, N)
                re_0 = jnp.where(first_8, p[:planes], rq[:planes])
                im_0 = jnp.where(first_8, rp[:planes], q[:planes]) * flip
                y_ref[0, 0, t] = jnp.where(top, re_0, re[:planes])
                y_ref[1, 0, t] = jnp.where(top, im_0, im[:planes])
        return carry

    lax.fori_loop(0, times // 8, z_step, 0)

    def t_group(g, lowest):
        for b in range(8):
            parts = transform([(y_ref[0, g, 8 * a + b], y_ref[1, g, 8 * a + b]) for a in range(16)])
            for c, v in enumerate(parts):
                re, im = turn_by(v, b * c, N)
                y_ref[0, g, 8 * c + b] = re
                y_ref[1, g, 8 * c + b] = im
        for c in range(9):
            spectrum = {}
            for k in {c, (16 - c) % 16}:
                parts = transform([(y_ref[0, g, 8 * k + b], y_ref[1, g, 8 * k + b]) for b in range(8)])
                for d, v in enumerate(parts):
                    spectrum[k + 16 * d] = v
            power = {k: re * re + im * im for k, (re, im) in spectrum.items()}
            for k in spectrum:
                ahead, back = power[k], power[(N - k) % N]
                here = jnp.where(straight, ahead, back)
                there = jnp.where(own_8, back, pltpu.roll(jnp.where(first_8, back, ahead), H, 1))
                if lowest:
                    upper = top & ~first_8
                    here, there = jnp.where(upper, there, here), jnp.where(upper, here, there)
                    (re, im), (re_m, im_m) = spectrum[k], spectrum[(N - k) % N]
                    one = (re + re_m) * (re + re_m) + (im - im_m) * (im - im_m)
                    two = (im + im_m) * (im + im_m) + (re - re_m) * (re - re_m)
                    one, two = one * 0.25, two * 0.25
                    mixed = jnp.where(first_8, two, one)
                    mixed = pltpu.roll(mixed, H, 1)
                    here = jnp.where(own_top, jnp.where(first_8, one, mixed), here)
                    there = jnp.where(own_top, jnp.where(first_8, mixed, two), there)
                o_ref[g, k] = here
                o_ref[gz - 1 - g, k, 1:, :] = there[1:]
                o_ref[groups if lowest else gz - g, k, :1, :] = there[:1]

    t_group(0, True)

    def t_step(g, carry):
        t_group(g, False)
        return carry

    lax.fori_loop(1, groups, t_step, 0)


def zt_transform(field, gz, ta):
    _, t, z, _ = field.shape
    field = field.reshape(gz, ta * t, z, N)
    return pl.pallas_call(
        zt_kernel,
        in_specs=[pl.BlockSpec(memory_space=pltpu.VMEM)] * 2,
        out_specs=pl.BlockSpec(memory_space=pltpu.VMEM),
        out_shape=jax.ShapeDtypeStruct((gz, N, z, N), F32),
        scratch_shapes=[pltpu.VMEM((2, gz // 2, N, z, N), F32)],
        compiler_params=pltpu.CompilerParams(vmem_limit_bytes=36 * MIB),
    )(field, jnp.asarray(table_z()))


def join_kernel(x_ref, o_ref, o_buf, o_sem):
    steps, z = o_ref.shape[:2]
    slots = o_buf.shape[0]
    falling = lax.axis_index("gz") >= lax.axis_size("gz") // 2
    lane = lane_of((z, N))
    back = (N + H - lane) % N

    def flush(t, slot):
        return [
            pltpu.make_async_copy(
                o_buf.at[slot, :, r, :],
                o_ref.at[t, jnp.where(falling, (z - r) % z, r)],
                o_sem.at[slot, r],
            )
            for r in range(z)
        ]

    def step(t, carry):
        slot = lax.rem(t, slots)

        @pl.when(t >= slots)
        def _():
            for copy in flush(t - slots, slot):
                copy.wait()

        for i in range(H):
            a, b = x_ref[i, t], x_ref[H + i, t]
            back_a = jnp.take_along_axis(a, back, axis=1)
            back_b = jnp.take_along_axis(b, back, axis=1)
            if i == 0:
                o_buf[slot, 0] = jnp.where(lane <= H, a, back_a)
                o_buf[slot, H] = jnp.where(lane <= H, b, back_b)
            else:
                o_buf[slot, i] = jnp.where(lane < H, a, back_b)
                o_buf[slot, N - i] = jnp.where((lane <= H) & (lane > 0), b, back_a)
        for copy in flush(t, slot):
            copy.start()
        return carry

    lax.fori_loop(0, steps, step, 0)
    for t in range(steps - slots, steps):
        for copy in flush(t, t % slots):
            copy.wait()


def join(received):
    _, t, z, _ = received.shape
    slots = 4
    return pl.pallas_call(
        join_kernel,
        in_specs=[pl.BlockSpec(memory_space=pltpu.VMEM)],
        out_specs=pl.BlockSpec(memory_space=pltpu.HBM),
        out_shape=jax.ShapeDtypeStruct((t, z, N, N), F32),
        scratch_shapes=[pltpu.VMEM((slots, N, z, N), F32), pltpu.SemaphoreType.DMA((slots, z))],
        compiler_params=pltpu.CompilerParams(vmem_limit_bytes=20 * MIB),
    )(received)


def body(potential):
    t, z, _, _ = potential.shape
    gz = lax.axis_size("gz")
    ta = lax.axis_size("ta")
    sent = xy_transform(potential)
    field = lax.all_to_all(sent, AXES, split_axis=0, concat_axis=0, tiled=True)
    power = zt_transform(field, gz, ta).reshape(gz * ta, t, z, N)
    received = lax.all_to_all(power, AXES, split_axis=0, concat_axis=0, tiled=True)
    return join(received)


def solution(mesh):
    return jax.shard_map(
        body,
        mesh=mesh,
        in_specs=(P("ta", "gz", None, None),),
        out_specs=P("ta", "gz", None, None),
        check_vma=False,
    )
```

time: 542 us -> 246 us (0.45); the launches traced: 533 us -> 245 us
  matrix products: 172 us -> 0 us
  blocking collectives: 308 us -> 214 us
  local copies, waits for them, and re-layouts: 42.9 us -> 0.91 us
  Pallas kernels: 0 us -> 30.4 us
  other arithmetic: 9.83 us -> 0 us
    dot_general x14 -> x0, matrix products: 172 us -> none  [the longest x3 43.3 us: rotate(): real_cos = jnp.einsum(form, real_part, cosine, precision=highest)]
    all_to_all x2, blocking collectives: 308 us -> 214 us  [the longest x1 109 us: body(): field = lax.all_to_all(sent, AXES, split_axis=0, concat_axis=0, tiled=True)]
    pallas_call x0 -> x3, Pallas kernels: none -> 30.4 us  [the longest x1 13.3 us: xy_transform(): pl.pallas_call(xy_kernel, in_specs=[pl.BlockSpec(memory_space=pltpu.HBM),...]
    transpose x2 -> x0, local copies, waits for them, and re-layouts: 24.7 us -> none  [the longest x1 17.7 us: spread_out(): moved = jnp.transpose(field, (2, 0, 1, 3))]
    reshape x1 -> x0, local copies, waits for them, and re-layouts: 9.95 us -> none  [bring_back(): blocks = values.reshape(groups_t, local_t, groups_z, local_z, rows_y, lanes)]
    transpose x1 -> x0, other arithmetic: 9.83 us -> none  [spread_out(): moved = jnp.transpose(field, (2, 0, 1, 3))]
    all_to_all x1 -> x0, local copies, waits for them, and re-layouts: 8.25 us -> none  [bring_back(): lax.all_to_all(blocks, ('gz', 'ta'), split_axis=0, concat_axis=2, tiled=T...]
where the time goes in v2:
time: 246 us; the launch traced here: 245 us
  blocking collectives  214 us (87%)
  Pallas kernels  30.4 us (12%)
    all_to_all x1, blocking collectives, body(): field = lax.all_to_all(sent, AXES, split_axis=0, concat_axis=0, tiled=True)  109 us
    all_to_all x1, blocking collectives, body(): lax.all_to_all(power, AXES, split_axis=0, concat_axis=0, tiled=True)  105 us
    pallas_call x1, Pallas kernels, xy_transform(): pl.pallas_call(xy_kernel, in_specs=[pl.BlockSpec(memory_space=pltpu.HBM),...  13.3 us
    pallas_call x1, Pallas kernels, zt_transform(): pl.pallas_call(zt_kernel, in_specs=[pl.BlockSpec(memory_space=pltpu.VMEM)...  12.2 us
    pallas_call x1, Pallas kernels, join(): pl.pallas_call(join_kernel, in_specs=[pl.BlockSpec(memory_space=pltpu.VME...  4.94 us

profile of v2, /device:TPU:1, one launch (start us, length us, event | category | flops | bytes accessed | tf_op | source)
XLA Modules:
  0.0 245.3 jit_solution(7418517981496300716)
XLA Ops:
  0.0 0.0 copy-start.1
  0.0 0.9 copy-done.1
  0.9 13.3 %shard_map.37 = f32[128,16,8,128]{3,2,1,0:T(8,128)} custom-call(f32[16,8,128,128]{3,2,1,0:T(8,128)} %x_ref.1, bf16[256,256]{1,0:T(8,128)(2,1)S(1)} %copy-done.1), custom_call_target="tpu_custom_call" | custom-call | tf_op jit(solution)/shard_map/pallas_call | solution.py:196
  14.2 0.0 copy-start
  14.2 109.5 %all_to_all.10 = f32[128,16,8,128]{3,2,1,0:T(8,128)S(1)} all-to-all(f32[128,16,8,128]{3,2,1,0:T(8,128)} %shard_map.37), channel_id=1, replica_groups=mesh['gz'=16,'ta'=8] {'gz','ta'}, dimensions={0} | all-to-all | bytes 16777216 | tf_op jit(solution)/shard_map/all_to_all | solution.py:371
  123.7 0.0 copy-done
  123.7 12.2 %shard_map.38 = f32[16,128,8,128]{3,2,1,0:T(8,128)S(1)} custom-call(f32[16,128,8,128]{3,2,1,0:T(8,128)S(1)} %bitcast.2, bf16[128,512]{1,0:T(8,128)(2,1)S(1)} %copy-done), custom_call_target="tpu_custom_call" | custom-call | tf_op jit(solution)/shard_map/pallas_call | solution.py:298
  135.9 104.5 %all_to_all.11.x_ref = f32[128,16,8,128]{3,2,1,0:T(8,128)S(1)} all-to-all(f32[128,16,8,128]{3,2,1,0:T(8,128)S(1)} %bitcast.3), channel_id=1, replica_groups=mesh['gz'=16,'ta'=8] {'gz','ta'}, dimensions={0} | all-to-all | bytes 16777216 | tf_op jit(solution)/shard_map/all_to_all | solution.py:373
  240.4 4.9 %shard_map.39 = f32[16,8,128,128]{3,2,1,0:T(8,128)} custom-call(f32[128,16,8,128]{3,2,1,0:T(8,128)S(1)} %all_to_all.11.x_ref), custom_call_target="tpu_custom_call" | custom-call | tf_op jit(solution)/shard_map/pallas_call | solution.py:356
Async XLA Ops:
  0.0 0.9 copy-start.1
  14.2 109.5 %copy-start = (bf16[128,512]{1,0:T(8,128)(2,1)S(1)}, bf16[128,512]{1,0:T(8,128)(2,1)}, u32[]{:S(2)}) copy-start(bf16[128,512]{1,0:T(8,128)(2,1)} %constant.5.clone.w_ref) | copy-start | bytes 393220

commit v3 on v2

--- a/solution.py
+++ b/solution.py
@@ -63,10 +63,6 @@
 def sub(a, b):
     im = a[1] if b[1] is None else -b[1] if a[1] is None else a[1] - b[1]
     return a[0] - b[0], im
-
-
-def conj(a):
-    return a[0], None if a[1] is None else -a[1]
 
 
 def turn_by(a, k, n):
@@ -87,6 +83,13 @@
     return re * c + im * s, im * c - re * s
 
 
+def butterfly(a, b, k, n):
+    if 4 * k == n and b[1] is not None and a[1] is not None:
+        return (a[0] + b[1], a[1] - b[0]), (a[0] - b[1], a[1] + b[0])
+    t = turn_by(b, k, n)
+    return add(a, t), sub(a, t)
+
+
 def transform(x):
     n = len(x)
     if n == 1:
@@ -94,8 +97,7 @@
     even, odd = transform(x[0::2]), transform(x[1::2])
     out = [None] * n
     for k in range(n // 2):
-        t = turn_by(odd[k], k, n)
-        out[k], out[k + n // 2] = add(even[k], t), sub(even[k], t)
+        out[k], out[k + n // 2] = butterfly(even[k], odd[k], k, n)
     return out
 
 
@@ -109,8 +111,8 @@
     out = [None] * (n // 2 + 1)
     out[0], out[n // 2] = add(even[0], odd[0]), sub(even[0], odd[0])
     for k in range(1, n // 4):
-        t = turn_by(odd[k], k, n)
-        out[k], out[n // 2 - k] = add(even[k], t), conj(sub(even[k], t))
+        (re, im), t = even[k], turn_by(odd[k], k, n)
+        out[k], out[n // 2 - k] = (re + t[0], im + t[1]), (re - t[0], t[1] - im)
     out[n // 4] = (even[n // 4][0], -odd[n // 4][0])
     return out
 
@@ -121,7 +123,6 @@
 
 def xy_kernel(x_ref, w_ref, o_ref, x_buf, f_buf, h_buf, x_sem):
     steps, planes = x_ref.shape[:2]
-    slots = x_buf.shape[0]
     lane = lane_of((planes, N))
     keep = jnp.where(lane == H, 0.0, 1.0).astype(F32)
     turn = jnp.where(lane == 0, 0.0, jnp.where(lane < H, -1.0, 1.0)).astype(F32)
@@ -129,22 +130,29 @@
     turn_back = jnp.where(lane < H, 1.0, -1.0).astype(F32)
     edge = lane == H
 
-    def fetch(t, slot):
-        return [
-            pltpu.make_async_copy(x_ref.at[t, z], x_buf.at[slot, :, z, :], x_sem.at[slot, z])
-            for z in range(planes)
-        ]
-
-    for t in range(slots):
-        for copy in fetch(t, t):
-            copy.start()
-
-    def step(t, carry):
-        slot = lax.rem(t, slots)
-        for copy in fetch(t, slot):
-            copy.wait()
+    def fetch(n):
+        for z in range(planes):
+            pltpu.make_async_copy(
+                x_ref.at[pl.ds(2 * n, 2), z], x_buf.at[pl.ds(2 * n, 2), :, z, :], x_sem.at[n]
+            ).start()
+
+    for n in range(2):
+        fetch(n)
+
+    def step(n, carry):
+        @pl.when(n + 2 < steps // 2)
+        def _():
+            fetch(n + 2)
+
+        whole = x_buf.at[pl.ds(2 * n, 2)]
+        pltpu.make_async_copy(whole, whole, x_sem.at[n]).wait()
+        for i in range(2):
+            plane(2 * n + i)
+        return carry
+
+    def plane(t):
         for b in range(8):
-            for c, v in enumerate(transform_real([x_buf[slot, 8 * a + b] for a in range(16)])):
+            for c, v in enumerate(transform_real([x_buf[t, 8 * a + b] for a in range(16)])):
                 re, im = turn_by(v, b * c, N)
                 h_buf[0, c, b] = re
                 if im is not None:
@@ -170,11 +178,6 @@
                 if ky % H:
                     f_buf[H + ky] = im
 
-        @pl.when(t + slots < steps)
-        def _():
-            for copy in fetch(t + slots, slot):
-                copy.start()
-
         hi, lo = split(f_buf[...].reshape(N * planes, N))
         r = jnp.dot(jnp.concatenate([hi, lo], axis=1), w_ref[...], preferred_element_type=F32)
         r = (r[:, :N] + r[:, N:]).reshape(N, planes, N)
@@ -185,26 +188,24 @@
             turned = pltpu.roll(jnp.where(edge, p, q), H, 1)
             o_ref[i, t] = p * keep + turned * turn
             o_ref[H + i, t] = jnp.where(edge, -q, p * keep_back + turned * turn_back)
-        return carry
-
-    lax.fori_loop(0, steps, step, 0)
+
+    lax.fori_loop(0, steps // 2, step, 0)
 
 
 def xy_transform(potential):
     t, z, _, _ = potential.shape
-    slots = 6
     return pl.pallas_call(
         xy_kernel,
         in_specs=[pl.BlockSpec(memory_space=pltpu.HBM), pl.BlockSpec(memory_space=pltpu.VMEM)],
         out_specs=pl.BlockSpec(memory_space=pltpu.VMEM),
         out_shape=jax.ShapeDtypeStruct((N, t, z, N), F32),
         scratch_shapes=[
-            pltpu.VMEM((slots, N, z, N), F32),
+            pltpu.VMEM((t, N, z, N), F32),
             pltpu.VMEM((N, z, N), F32),
             pltpu.VMEM((2, 9, 8, z, N), F32),
-            pltpu.SemaphoreType.DMA((slots, z)),
+            pltpu.SemaphoreType.DMA((t // 2,)),
         ],
-        compiler_params=pltpu.CompilerParams(vmem_limit_bytes=48 * MIB),
+        compiler_params=pltpu.CompilerParams(vmem_limit_bytes=42 * MIB),
     )(potential, jnp.asarray(table_x()))
 
 
@@ -230,12 +231,12 @@
     straight = first_8 | own_8
 
     def z_step(n, carry):
-        for m in range(0, 8, 2):
-            his, los = zip(*[split(x_ref[:, 8 * n + m + i].reshape(gz * planes, N)) for i in range(2)])
+        for m in range(0, 32, 2):
+            his, los = zip(*[split(x_ref[:, 32 * n + m + i].reshape(gz * planes, N)) for i in range(2)])
             hi, lo = jnp.concatenate(his, axis=1), jnp.concatenate(los, axis=1)
             out = jnp.dot(w_ref[...], jnp.concatenate([hi, lo, hi, lo], axis=0), preferred_element_type=F32)
             for i in range(2):
-                t = 8 * n + m + i
+                t = 32 * n + m + i
                 p, q = out[:H, N * i : N * i + N], out[H:, N * i : N * i + N]
                 rp, rq = pltpu.roll(p, H, 1), pltpu.roll(q, H, 1)
                 u, v = p * u_p + rq * u_q, rp * v_p - q * v_q
@@ -248,7 +249,7 @@
                 y_ref[1, 0, t] = jnp.where(top, im_0, im[:planes])
         return carry
 
-    lax.fori_loop(0, times // 8, z_step, 0)
+    lax.fori_loop(0, times // 32, z_step, 0)
 
     def t_group(g, lowest):
         for b in range(8):
@@ -307,58 +308,39 @@
 
 def join_kernel(x_ref, o_ref, o_buf, o_sem):
     steps, z = o_ref.shape[:2]
-    slots = o_buf.shape[0]
     falling = lax.axis_index("gz") >= lax.axis_size("gz") // 2
     lane = lane_of((z, N))
     back = (N + H - lane) % N
 
-    def flush(t, slot):
-        return [
-            pltpu.make_async_copy(
-                o_buf.at[slot, :, r, :],
-                o_ref.at[t, jnp.where(falling, (z - r) % z, r)],
-                o_sem.at[slot, r],
-            )
-            for r in range(z)
-        ]
-
     def step(t, carry):
-        slot = lax.rem(t, slots)
-
-        @pl.when(t >= slots)
-        def _():
-            for copy in flush(t - slots, slot):
-                copy.wait()
-
         for i in range(H):
             a, b = x_ref[i, t], x_ref[H + i, t]
             back_a = jnp.take_along_axis(a, back, axis=1)
             back_b = jnp.take_along_axis(b, back, axis=1)
             if i == 0:
-                o_buf[slot, 0] = jnp.where(lane <= H, a, back_a)
-                o_buf[slot, H] = jnp.where(lane <= H, b, back_b)
+                o_buf[t, 0] = jnp.where(lane <= H, a, back_a)
+                o_buf[t, H] = jnp.where(lane <= H, b, back_b)
             else:
-                o_buf[slot, i] = jnp.where(lane < H, a, back_b)
-                o_buf[slot, N - i] = jnp.where((lane <= H) & (lane > 0), b, back_a)
-        for copy in flush(t, slot):
-            copy.start()
+                o_buf[t, i] = jnp.where(lane < H, a, back_b)
+                o_buf[t, N - i] = jnp.where((lane <= H) & (lane > 0), b, back_a)
+        for r in range(z):
+            pltpu.make_async_copy(
+                o_buf.at[t, :, r, :], o_ref.at[t, jnp.where(falling, (z - r) % z, r)], o_sem
+            ).start()
         return carry
 
     lax.fori_loop(0, steps, step, 0)
-    for t in range(steps - slots, steps):
-        for copy in flush(t, t % slots):
-            copy.wait()
+    pltpu.make_async_copy(o_buf, o_buf, o_sem).wait()
 
 
 def join(received):
     _, t, z, _ = received.shape
-    slots = 4
     return pl.pallas_call(
         join_kernel,
         in_specs=[pl.BlockSpec(memory_space=pltpu.VMEM)],
         out_specs=pl.BlockSpec(memory_space=pltpu.HBM),
         out_shape=jax.ShapeDtypeStruct((t, z, N, N), F32),
-        scratch_shapes=[pltpu.VMEM((slots, N, z, N), F32), pltpu.SemaphoreType.DMA((slots, z))],
+        scratch_shapes=[pltpu.VMEM((t, N, z, N), F32), pltpu.SemaphoreType.DMA],
         compiler_params=pltpu.CompilerParams(vmem_limit_bytes=20 * MIB),
     )(received)
 

time: 246 us -> 237 us (0.963)
  Pallas kernels: 30.4 us -> 21.9 us
    pallas_call x1, Pallas kernels: 13.3 us -> 8.29 us  [xy_transform(): pl.pallas_call(xy_kernel, in_specs=[pl.BlockSpec(memory_space=pltpu.HBM),...]
    pallas_call x1, Pallas kernels: 12.2 us -> 9.44 us  [zt_transform(): pl.pallas_call(zt_kernel, in_specs=[pl.BlockSpec(memory_space=pltpu.VMEM)...]
where the time goes in v3:
time: 237 us
  blocking collectives  214 us (90%)
  Pallas kernels  21.9 us (9%)
    all_to_all x1, blocking collectives, body(): field = lax.all_to_all(sent, AXES, split_axis=0, concat_axis=0, tiled=True)  109 us
    all_to_all x1, blocking collectives, body(): lax.all_to_all(power, AXES, split_axis=0, concat_axis=0, tiled=True)  105 us
    pallas_call x1, Pallas kernels, zt_transform(): pl.pallas_call(zt_kernel, in_specs=[pl.BlockSpec(memory_space=pltpu.VMEM)...  9.44 us
    pallas_call x1, Pallas kernels, xy_transform(): pl.pallas_call(xy_kernel, in_specs=[pl.BlockSpec(memory_space=pltpu.HBM),...  8.29 us

profile of v3, /device:TPU:1, one launch (start us, length us, event | category | flops | bytes accessed | tf_op | source)
XLA Modules:
  0.0 236.6 jit_solution(18174061030178139439)
XLA Ops:
  0.0 0.0 copy-start.1
  0.0 0.9 copy-done.1
  0.9 8.3 %shard_map.37 = f32[128,16,8,128]{3,2,1,0:T(8,128)S(1)} custom-call(f32[16,8,128,128]{3,2,1,0:T(8,128)} %x_ref.1, bf16[256,256]{1,0:T(8,128)(2,1)S(1)} %copy-done.1), custom_call_target="tpu_custom_call" | custom-call | tf_op jit(solution)/shard_map/pallas_call | solution.py:197
  9.2 0.0 copy-start
  9.2 109.2 %all_to_all.10 = f32[128,16,8,128]{3,2,1,0:T(8,128)S(1)} all-to-all(f32[128,16,8,128]{3,2,1,0:T(8,128)S(1)} %shard_map.37), channel_id=1, replica_groups=mesh['gz'=16,'ta'=8] {'gz','ta'}, dimensions={0} | all-to-all | bytes 16777216 | tf_op jit(solution)/shard_map/all_to_all | solution.py:353
  118.4 0.0 copy-done
  118.5 9.4 %shard_map.38 = f32[16,128,8,128]{3,2,1,0:T(8,128)S(1)} custom-call(f32[16,128,8,128]{3,2,1,0:T(8,128)S(1)} %bitcast.2, bf16[128,512]{1,0:T(8,128)(2,1)S(1)} %copy-done), custom_call_target="tpu_custom_call" | custom-call | tf_op jit(solution)/shard_map/pallas_call | solution.py:299
  127.9 104.5 %all_to_all.11.x_ref = f32[128,16,8,128]{3,2,1,0:T(8,128)S(1)} all-to-all(f32[128,16,8,128]{3,2,1,0:T(8,128)S(1)} %bitcast.3), channel_id=1, replica_groups=mesh['gz'=16,'ta'=8] {'gz','ta'}, dimensions={0} | all-to-all | bytes 16777216 | tf_op jit(solution)/shard_map/all_to_all | solution.py:355
  232.4 4.1 %shard_map.39 = f32[16,8,128,128]{3,2,1,0:T(8,128)} custom-call(f32[128,16,8,128]{3,2,1,0:T(8,128)S(1)} %all_to_all.11.x_ref), custom_call_target="tpu_custom_call" | custom-call | tf_op jit(solution)/shard_map/pallas_call | solution.py:338
Async XLA Ops:
  0.0 0.9 copy-start.1
  9.2 109.3 %copy-start = (bf16[128,512]{1,0:T(8,128)(2,1)S(1)}, bf16[128,512]{1,0:T(8,128)(2,1)}, u32[]{:S(2)}) copy-start(bf16[128,512]{1,0:T(8,128)(2,1)} %constant.5.clone.w_ref) | copy-start | bytes 393220

commit v4 on v3

--- a/solution.py
+++ b/solution.py
@@ -35,12 +35,19 @@
 
 
 def table_x():
-    c, s = angles()
-    w = np.concatenate([c[:, :H], -s[:, :H]], axis=1)
-    w[:, H] = c[:, H]
-    hi, lo = split_np(w / N)
-    row = np.concatenate([hi, lo], axis=1)
-    return np.concatenate([row, row], axis=0)
+    x = lax.broadcasted_iota(jnp.int32, (N, N), 0)
+    lane = lane_of((N, N))
+    k = jnp.where(lane <= H, lane, lane - H)
+    phase = (x * k + jnp.where(lane > H, N // 4, 0)) % N
+    v = (phase - H).astype(F32) * float(np.pi / N)
+    v2 = v * v
+    sine = jnp.full((N, N), 1.0 / 6227020800.0, F32)
+    for c in (-1.0 / 39916800, 1.0 / 362880, -1.0 / 5040, 1.0 / 120, -1.0 / 6, 1.0):
+        sine = sine * v2 + c
+    sine = sine * v
+    hi, lo = split((2.0 * sine * sine - 1.0) * (1.0 / N))
+    row = jnp.concatenate([hi, lo], axis=1)
+    return jnp.concatenate([row, row], axis=0)
 
 
 def table_z():
@@ -121,7 +128,7 @@
     return lax.broadcasted_iota(jnp.int32, shape, 1)
 
 
-def xy_kernel(x_ref, w_ref, o_ref, x_buf, f_buf, h_buf, x_sem):
+def xy_kernel(x_ref, o_ref, w_ref, x_buf, f_buf, h_buf, x_sem):
     steps, planes = x_ref.shape[:2]
     lane = lane_of((planes, N))
     keep = jnp.where(lane == H, 0.0, 1.0).astype(F32)
@@ -136,14 +143,11 @@
                 x_ref.at[pl.ds(2 * n, 2), z], x_buf.at[pl.ds(2 * n, 2), :, z, :], x_sem.at[n]
             ).start()
 
-    for n in range(2):
+    for n in range(steps // 2):
         fetch(n)
+    w_ref[...] = table_x()
 
     def step(n, carry):
-        @pl.when(n + 2 < steps // 2)
-        def _():
-            fetch(n + 2)
-
         whole = x_buf.at[pl.ds(2 * n, 2)]
         pltpu.make_async_copy(whole, whole, x_sem.at[n]).wait()
         for i in range(2):
@@ -196,17 +200,18 @@
     t, z, _, _ = potential.shape
     return pl.pallas_call(
         xy_kernel,
-        in_specs=[pl.BlockSpec(memory_space=pltpu.HBM), pl.BlockSpec(memory_space=pltpu.VMEM)],
+        in_specs=[pl.BlockSpec(memory_space=pltpu.HBM)],
         out_specs=pl.BlockSpec(memory_space=pltpu.VMEM),
         out_shape=jax.ShapeDtypeStruct((N, t, z, N), F32),
         scratch_shapes=[
+            pltpu.VMEM((2 * N, 2 * N), BF),
             pltpu.VMEM((t, N, z, N), F32),
             pltpu.VMEM((N, z, N), F32),
             pltpu.VMEM((2, 9, 8, z, N), F32),
             pltpu.SemaphoreType.DMA((t // 2,)),
         ],
         compiler_params=pltpu.CompilerParams(vmem_limit_bytes=42 * MIB),
-    )(potential, jnp.asarray(table_x()))
+    )(potential)
 
 
 def zt_kernel(x_ref, w_ref, o_ref, y_ref):
@@ -231,12 +236,12 @@
     straight = first_8 | own_8
 
     def z_step(n, carry):
-        for m in range(0, 32, 2):
-            his, los = zip(*[split(x_ref[:, 32 * n + m + i].reshape(gz * planes, N)) for i in range(2)])
+        for m in range(0, 64, 2):
+            his, los = zip(*[split(x_ref[:, 64 * n + m + i].reshape(gz * planes, N)) for i in range(2)])
             hi, lo = jnp.concatenate(his, axis=1), jnp.concatenate(los, axis=1)
             out = jnp.dot(w_ref[...], jnp.concatenate([hi, lo, hi, lo], axis=0), preferred_element_type=F32)
             for i in range(2):
-                t = 32 * n + m + i
+                t = 64 * n + m + i
                 p, q = out[:H, N * i : N * i + N], out[H:, N * i : N * i + N]
                 rp, rq = pltpu.roll(p, H, 1), pltpu.roll(q, H, 1)
                 u, v = p * u_p + rq * u_q, rp * v_p - q * v_q
@@ -249,7 +254,7 @@
                 y_ref[1, 0, t] = jnp.where(top, im_0, im[:planes])
         return carry
 
-    lax.fori_loop(0, times // 32, z_step, 0)
+    lax.fori_loop(0, times // 64, z_step, 0)
 
     def t_group(g, lowest):
         for b in range(8):

time: 237 us -> 235 us (level)
  no operation moved by 1% of the time
where the time goes in v4:
time: 235 us
  blocking collectives  214 us (91%)
  Pallas kernels  21.5 us (9%)
    all_to_all x1, blocking collectives, body(): field = lax.all_to_all(sent, AXES, split_axis=0, concat_axis=0, tiled=True)  109 us
    all_to_all x1, blocking collectives, body(): lax.all_to_all(power, AXES, split_axis=0, concat_axis=0, tiled=True)  105 us
    pallas_call x1, Pallas kernels, zt_transform(): pl.pallas_call(zt_kernel, in_specs=[pl.BlockSpec(memory_space=pltpu.VMEM)...  9.28 us
    pallas_call x1, Pallas kernels, xy_transform(): pl.pallas_call(xy_kernel, in_specs=[pl.BlockSpec(memory_space=pltpu.HBM)]...  8.06 us

profile of v4, /device:TPU:1, one launch (start us, length us, event | category | flops | bytes accessed | tf_op | source)
XLA Modules:
  0.0 235.2 jit_solution(10759248151608176581)
XLA Ops:
  0.0 8.1 %shard_map.28 = f32[128,16,8,128]{3,2,1,0:T(8,128)S(1)} custom-call(f32[16,8,128,128]{3,2,1,0:T(8,128)} %x_ref.1), custom_call_target="tpu_custom_call" | custom-call | tf_op jit(solution)/shard_map/pallas_call | solution.py:201
  8.1 0.0 copy-start
  8.1 109.2 %all_to_all.10 = f32[128,16,8,128]{3,2,1,0:T(8,128)S(1)} all-to-all(f32[128,16,8,128]{3,2,1,0:T(8,128)S(1)} %shard_map.28), channel_id=1, replica_groups=mesh['gz'=16,'ta'=8] {'gz','ta'}, dimensions={0} | all-to-all | bytes 16777216 | tf_op jit(solution)/shard_map/all_to_all | solution.py:358
  117.3 0.0 copy-done
  117.3 9.3 %shard_map.29 = f32[16,128,8,128]{3,2,1,0:T(8,128)S(1)} custom-call(f32[16,128,8,128]{3,2,1,0:T(8,128)S(1)} %bitcast.2, bf16[128,512]{1,0:T(8,128)(2,1)S(1)} %copy-done), custom_call_target="tpu_custom_call" | custom-call | tf_op jit(solution)/shard_map/pallas_call | solution.py:304
  126.6 104.5 %all_to_all.11.x_ref = f32[128,16,8,128]{3,2,1,0:T(8,128)S(1)} all-to-all(f32[128,16,8,128]{3,2,1,0:T(8,128)S(1)} %bitcast.3), channel_id=1, replica_groups=mesh['gz'=16,'ta'=8] {'gz','ta'}, dimensions={0} | all-to-all | bytes 16777216 | tf_op jit(solution)/shard_map/all_to_all | solution.py:360
  231.1 4.1 %shard_map.30 = f32[16,8,128,128]{3,2,1,0:T(8,128)} custom-call(f32[128,16,8,128]{3,2,1,0:T(8,128)S(1)} %all_to_all.11.x_ref), custom_call_target="tpu_custom_call" | custom-call | tf_op jit(solution)/shard_map/pallas_call | solution.py:343
Async XLA Ops:
  8.1 109.3 %copy-start = (bf16[128,512]{1,0:T(8,128)(2,1)S(1)}, bf16[128,512]{1,0:T(8,128)(2,1)}, u32[]{:S(2)}) copy-start(bf16[128,512]{1,0:T(8,128)(2,1)} %constant.2.clone.w_ref) | copy-start | bytes 393220

commit v5 on v4

--- a/solution.py
+++ b/solution.py
@@ -128,7 +128,7 @@
     return lax.broadcasted_iota(jnp.int32, shape, 1)
 
 
-def xy_kernel(x_ref, o_ref, w_ref, x_buf, f_buf, h_buf, x_sem):
+def xy_kernel(x_ref, o_ref, w_ref, x_buf, f_bufs, h_bufs, x_sem):
     steps, planes = x_ref.shape[:2]
     lane = lane_of((planes, N))
     keep = jnp.where(lane == H, 0.0, 1.0).astype(F32)
@@ -151,10 +151,10 @@
         whole = x_buf.at[pl.ds(2 * n, 2)]
         pltpu.make_async_copy(whole, whole, x_sem.at[n]).wait()
         for i in range(2):
-            plane(2 * n + i)
+            plane(2 * n + i, f_bufs.at[i], h_bufs.at[i])
         return carry
 
-    def plane(t):
+    def plane(t, f_buf, h_buf):
         for b in range(8):
             for c, v in enumerate(transform_real([x_buf[t, 8 * a + b] for a in range(16)])):
                 re, im = turn_by(v, b * c, N)
@@ -206,8 +206,8 @@
         scratch_shapes=[
             pltpu.VMEM((2 * N, 2 * N), BF),
             pltpu.VMEM((t, N, z, N), F32),
-            pltpu.VMEM((N, z, N), F32),
-            pltpu.VMEM((2, 9, 8, z, N), F32),
+            pltpu.VMEM((2, N, z, N), F32),
+            pltpu.VMEM((2, 2, 9, 8, z, N), F32),
             pltpu.SemaphoreType.DMA((t // 2,)),
         ],
         compiler_params=pltpu.CompilerParams(vmem_limit_bytes=42 * MIB),
@@ -292,10 +292,12 @@
     t_group(0, True)
 
     def t_step(g, carry):
-        t_group(g, False)
+        t_group(2 * g + 1, False)
+        t_group(2 * g + 2, False)
         return carry
 
-    lax.fori_loop(1, groups, t_step, 0)
+    lax.fori_loop(0, groups // 2 - 1, t_step, 0)
+    t_group(groups - 1, False)
 
 
 def zt_transform(field, gz, ta):

time: 235 us -> 235 us (level)
  no operation moved by 1% of the time
where the time goes in v5:
time: 235 us
  blocking collectives  214 us (91%)
  Pallas kernels  21.3 us (9%)
    all_to_all x1, blocking collectives, body(): field = lax.all_to_all(sent, AXES, split_axis=0, concat_axis=0, tiled=True)  109 us
    all_to_all x1, blocking collectives, body(): lax.all_to_all(power, AXES, split_axis=0, concat_axis=0, tiled=True)  105 us
    pallas_call x1, Pallas kernels, zt_transform(): pl.pallas_call(zt_kernel, in_specs=[pl.BlockSpec(memory_space=pltpu.VMEM)...  9.08 us
    pallas_call x1, Pallas kernels, xy_transform(): pl.pallas_call(xy_kernel, in_specs=[pl.BlockSpec(memory_space=pltpu.HBM)]...  8.06 us

profile of v5, /device:TPU:1, one launch (start us, length us, event | category | flops | bytes accessed | tf_op | source)
XLA Modules:
  0.0 235.1 jit_solution(16904424528547961605)
XLA Ops:
  0.0 8.1 %shard_map.28 = f32[128,16,8,128]{3,2,1,0:T(8,128)S(1)} custom-call(f32[16,8,128,128]{3,2,1,0:T(8,128)} %x_ref.1), custom_call_target="tpu_custom_call" | custom-call | tf_op jit(solution)/shard_map/pallas_call | solution.py:201
  8.1 0.0 copy-start
  8.1 109.2 %all_to_all.10 = f32[128,16,8,128]{3,2,1,0:T(8,128)S(1)} all-to-all(f32[128,16,8,128]{3,2,1,0:T(8,128)S(1)} %shard_map.28), channel_id=1, replica_groups=mesh['gz'=16,'ta'=8] {'gz','ta'}, dimensions={0} | all-to-all | bytes 16777216 | tf_op jit(solution)/shard_map/all_to_all | solution.py:360
  117.3 0.0 copy-done
  117.3 9.1 %shard_map.29 = f32[16,128,8,128]{3,2,1,0:T(8,128)S(1)} custom-call(f32[16,128,8,128]{3,2,1,0:T(8,128)S(1)} %bitcast.2, bf16[128,512]{1,0:T(8,128)(2,1)S(1)} %copy-done), custom_call_target="tpu_custom_call" | custom-call | tf_op jit(solution)/shard_map/pallas_call | solution.py:306
  126.4 104.5 %all_to_all.11.x_ref = f32[128,16,8,128]{3,2,1,0:T(8,128)S(1)} all-to-all(f32[128,16,8,128]{3,2,1,0:T(8,128)S(1)} %bitcast.3), channel_id=1, replica_groups=mesh['gz'=16,'ta'=8] {'gz','ta'}, dimensions={0} | all-to-all | bytes 16777216 | tf_op jit(solution)/shard_map/all_to_all | solution.py:362
  230.9 4.1 %shard_map.30 = f32[16,8,128,128]{3,2,1,0:T(8,128)} custom-call(f32[128,16,8,128]{3,2,1,0:T(8,128)S(1)} %all_to_all.11.x_ref), custom_call_target="tpu_custom_call" | custom-call | tf_op jit(solution)/shard_map/pallas_call | solution.py:345
Async XLA Ops:
  8.1 109.3 %copy-start = (bf16[128,512]{1,0:T(8,128)(2,1)S(1)}, bf16[128,512]{1,0:T(8,128)(2,1)}, u32[]{:S(2)}) copy-start(bf16[128,512]{1,0:T(8,128)(2,1)} %constant.2.clone.w_ref) | copy-start | bytes 393220
